TPU v7x, 32 devices: a whole 2x2x4 slice. The times are simulated.
32 devices in a mesh: row: 4 (over z), col: 8 (over y, x, core).
Axes of the slice: x: 2, y: 2, z: 4, core: 2. Of those that a mesh axis runs over, the one named last changes fastest.
Arguments:
- a_matrix: float32 [1024, 3072], P('row', 'col'), may hold values from -6 to 6
- b_matrix: float32 [1024, 3072], P('row', 'col'), as said below
Outputs:
- a_result: float32 [1024, 3072], P('row', 'col')
- b_result: float32 [1024, 3072], P('row', 'col')
Inputs may be any that keep to these rules, and one draw needn't show every extreme that they name: b_matrix is zero in its first 256 columns and, at the window's columns t, zero in rows below t; its entry in row t at window column t lies between 4 and 8.
All inputs are finite; a program needn't handle non-finite values.
Results may differ from a plain program's by a relative error of at most 0.00023.
Values sent between devices are 32-bit elements; how exact they have to be, the bound alone decides.
A program may use at most 64 MiB of HBM per device.

v0:
```python
import jax
import jax.numpy as jnp
from jax import lax
from jax.sharding import PartitionSpec as P

NB = 256


def broadcast(block, axis, source):
    block = jnp.where(lax.axis_index(axis) == source, block, jnp.zeros_like(block))
    return lax.psum(block, axis)


def product(left_side, right_side):
    return jnp.dot(
        left_side, right_side, precision=lax.Precision.HIGHEST, preferred_element_type=jnp.float32
    )


def tri_solve(factor, values, on_left, transpose):
    return lax.linalg.triangular_solve(
        factor, values, left_side=on_left, lower=True, transpose_a=transpose
    )


def inverse_of(square):
    normal = product(square.T, square)
    factor = jnp.linalg.cholesky(normal)
    first = tri_solve(factor, square.T, True, False)
    return tri_solve(factor, first, True, True)


def lower_from_reversed(gram):
    factor = jnp.linalg.cholesky(gram[::-1, ::-1])
    return factor.T[::-1, ::-1]


def local(a_matrix, b_matrix):
    panel_width = NB
    block_cols = a_matrix.shape[1]
    row_count = lax.axis_size("row")
    window_rows = panel_width * row_count
    window_dev = window_rows // lax.axis_size("col")
    identity = jnp.eye(panel_width, dtype=jnp.float32)
    row_place = lax.axis_index("row")
    col_place = lax.axis_index("col")
    top_flag = (row_place == 0).astype(jnp.float32)
    panel = broadcast(a_matrix[:, :panel_width], "col", 0)
    gram, top_panel = lax.psum((product(panel.T, panel), panel * top_flag), "row")
    factor = jnp.linalg.cholesky(gram)
    q_rows = tri_solve(factor, panel, False, True)
    q_top = tri_solve(factor, top_panel, False, True)
    w_rows = q_rows + top_flag * identity
    sums_a, sums_b = lax.psum((product(w_rows.T, a_matrix), product(w_rows.T, b_matrix)), "row")
    left_inverse = inverse_of(identity + q_top)
    a_left = a_matrix - product(w_rows, product(left_inverse, sums_a))
    b_left = b_matrix - product(w_rows, product(left_inverse, sums_b))
    strip_block = broadcast(b_left, "row", row_count - 1)
    local_cols = jnp.arange(block_cols)
    start_local = block_cols - window_dev
    inside = local_cols >= start_local
    in_window = inside.astype(jnp.float32)
    position = col_place * window_dev + local_cols - start_local
    last_pos = position - (window_rows - panel_width)
    picked = ((jnp.arange(panel_width)[:, None] == last_pos[None, :]) & inside[None, :]).astype(
        jnp.float32
    )
    strip_masked = strip_block * in_window[None, :]
    z_a, z_b, gram_right, strip_last, a_last, b_last = lax.psum(
        (
            product(a_left, strip_masked.T),
            product(b_left, strip_masked.T),
            product(strip_masked, strip_masked.T),
            product(strip_block, picked.T),
            product(a_left, picked.T),
            product(b_left, picked.T),
        ),
        "col",
    )
    right_factor = lower_from_reversed(gram_right)
    q_last = tri_solve(right_factor, strip_last.T, False, False)
    right_inverse = inverse_of(identity + q_last.T)
    w_cols = tri_solve(right_factor, strip_masked, True, True) + picked
    coeff_a = product(tri_solve(right_factor, z_a, False, False) + a_last, right_inverse)
    coeff_b = product(tri_solve(right_factor, z_b, False, False) + b_last, right_inverse)
    a_result = a_left - product(coeff_a, w_cols)
    b_result = b_left - product(coeff_b, w_cols)
    return (a_result, b_result)


def solution(mesh):
    placed = (P("row", "col"), P("row", "col"))
    return jax.shard_map(
        local,
        mesh=mesh,
        in_specs=placed,
        out_specs=(P("row", "col"), P("row", "col")),
        check_vma=False,
    )
```

profile of v0, /device:TPU:0, one launch (start us, length us, event | category | flops | bytes accessed | tf_op | source)
XLA Modules:
  0.0 532.9 jit_solution(867962301768831684)
XLA Ops:
  7.2 0.9 slice-done
  8.3 0.7 broadcast_select_fusion.1
  9.1 58.8 %all-reduce.10.cloned.1.call-done = f32[256,256]{0,1:T(8,128)} async-done(((f32[256,256]{0,1:T(8,128)}), f32[256,256]{0,1:T(8,128)}) %all-reduce.10.cloned.1.call-update) | async-done | bytes 262160 | tf_op jit(solution)/shard_map/psum | solution.py:11
  67.9 2.1 fusion.99
  70.1 0.9 copy-done
  71.0 0.7 broadcast_multiply_fusion.1
  71.7 33.9 %all-reduce.12.cloned.1.call-done = f32[256,256]{0,1:T(8,128)} async-done(((f32[256,256]{0,1:T(8,128)}), f32[256,256]{0,1:T(8,128)}) %all-reduce.12.cloned.1.call-update) | async-done | bytes 262160 | tf_op jit(solution)/shard_map/psum | solution.py:49
  105.6 1.1 copy.6
  106.8 11.7 %cholesky.214 = f32[128,128]{1,0:T(8,128)S(1)} custom-call(f32[128,128]{1,0:T(8,128)S(1)} %cholesky.346), custom_call_target="Cholesky" | custom-call | tf_op jit(solution)/shard_map/jit(cholesky)/cholesky | solution.py:50
  118.6 9.8 %custom-call.32 = f32[1,128,128]{1,2,0:T(8,128)S(1)} custom-call(f32[1,128,128]{2,1,0:T(8,128)S(1)} %get-tuple-element.167), custom_call_target="InvertDiagBlocksLowerTriangular" | custom-call | tf_op jit(solution)/shard_map/jit(cholesky)/cholesky | solution.py:50
  128.9 11.7 %cholesky.231 = f32[128,128]{1,0:T(8,128)S(1)} custom-call(f32[128,128]{1,0:T(8,128)S(1)} %convolution_subtract_fusion.17), custom_call_target="Cholesky" | custom-call | tf_op jit(solution)/shard_map/jit(cholesky)/cholesky | solution.py:50
  140.7 0.7 compare_reduce_fusion.6
  142.9 4.3 while.19
  143.7 1.4 bitcast_dynamic-update-slice_fusion.8
  145.8 1.4 bitcast_dynamic-update-slice_fusion.8
  147.2 19.7 %custom-call.33 = f32[2,128,128]{1,2,0:T(8,128)S(1)} custom-call(f32[2,128,128]{2,1,0:T(8,128)S(1)} %get-tuple-element.77), custom_call_target="InvertDiagBlocksLowerTriangular" | custom-call | tf_op jit(solution)/shard_map/triangular_solve/custom-call.0 | solution.py:21
  168.2 1.4 fusion.93
  169.6 0.9 copy-done.1
  170.6 1.4 fusion.94
  171.9 38.3 %all-reduce.18.cloned.1.call-done = (f32[256,256]{0,1:T(8,128)}, f32[256,384]{1,0:T(8,128)}) async-done(((f32[256,256]{0,1:T(8,128)}, f32[256,384]{1,0:T(8,128)}), (f32[256,256]{0,1:T(8,128)}, f32[256,384]{1,0:T(8,128)})) %all-reduce.18.cloned.1.call-update) | async-done | bytes 655376 | tf_op jit(solution)/shard_map/psum | solution.py:49
  210.2 1.3 fusion.46
  212.8 11.7 %cholesky.248 = f32[128,128]{1,0:T(8,128)S(1)} custom-call(f32[128,128]{1,0:T(8,128)S(1)} %cholesky.349), custom_call_target="Cholesky" | custom-call | tf_op jit(solution)/shard_map/jit(cholesky)/cholesky | solution.py:28
  224.6 9.8 %custom-call.35 = f32[1,128,128]{1,2,0:T(8,128)S(1)} custom-call(f32[1,128,128]{2,1,0:T(8,128)S(1)} %get-tuple-element.163), custom_call_target="InvertDiagBlocksLowerTriangular" | custom-call | tf_op jit(solution)/shard_map/jit(cholesky)/cholesky | solution.py:28
  234.8 11.7 %cholesky.265 = f32[128,128]{1,0:T(8,128)S(1)} custom-call(f32[128,128]{1,0:T(8,128)S(1)} %convolution_subtract_fusion.16), custom_call_target="Cholesky" | custom-call | tf_op jit(solution)/shard_map/jit(cholesky)/cholesky | solution.py:28
  246.6 0.7 compare_reduce_fusion.4
  247.3 0.6 compare_reduce_fusion.5
  249.3 4.4 while.20
  250.3 1.4 bitcast_dynamic-update-slice_fusion.9
  252.3 1.4 bitcast_dynamic-update-slice_fusion.9
  253.7 19.7 %custom-call.37 = f32[2,128,128]{1,2,0:T(8,128)S(1)} custom-call(f32[2,128,128]{2,1,0:T(8,128)S(1)} %get-tuple-element.80), custom_call_target="InvertDiagBlocksLowerTriangular" | custom-call | tf_op jit(solution)/shard_map/triangular_solve/custom-call.5 | solution.py:21
  276.1 1.4 broadcast_select_fusion
  277.7 1.1 fusion.1
  278.8 42.4 %all-reduce.16.cloned.1.call-done = (f32[256,384]{1,0:T(8,128)}, f32[256,384]{1,0:T(8,128)}) async-done(((f32[256,384]{1,0:T(8,128)}, f32[256,384]{1,0:T(8,128)}), (f32[256,384]{1,0:T(8,128)}, f32[256,384]{1,0:T(8,128)})) %all-reduce.16.cloned.1.call-update) | async-done | bytes 786448 | tf_op jit(solution)/shard_map/psum | solution.py:54
  321.2 1.0 broadcast_multiply_fusion
  322.2 1.3 fusion.102
  324.1 0.6 convolution_subtract_fusion.3
  324.8 1.3 fusion.100
  326.1 1.1 fusion.5
  328.2 1.1 fusion.3
  329.3 1.7 rev.6
  331.1 59.9 %all-reduce.14.cloned.1.call-done = (f32[256,256]{0,1:T(8,128)}, f32[256,256]{1,0:T(8,128)}, f32[256,256]{0,1:T(8,128)}, f32[256,256]{1,0:T(8,128)}, f32[256,256]{0,1:T(8,128)}, /*index=5*/f32[256,256]{1,0:T(8,128)}) async-done(((f32[256,256]{0,1:T(8,128)}, f32[256,256]{1,0:T(8,128)}, f32[256,256]{0,1:T(8,128)}, f32[256,256]{1,0:T(8,128)}, f32[256,256]{0,1:T(8,128)}, /*index=5*/f32[256,256]{1,0:T(8,128)}), ...) | async-done | bytes 1572880 | tf_op jit(solution)/shard_map/psum | solution.py:69
  391.0 1.1 copy.9
  392.2 11.7 %cholesky.282 = f32[128,128]{1,0:T(8,128)S(1)} custom-call(f32[128,128]{1,0:T(8,128)S(1)} %cholesky.352), custom_call_target="Cholesky" | custom-call | tf_op jit(solution)/shard_map/jit(cholesky)/cholesky | solution.py:34
  404.0 9.8 %custom-call.38 = f32[1,128,128]{1,2,0:T(8,128)S(1)} custom-call(f32[1,128,128]{2,1,0:T(8,128)S(1)} %get-tuple-element.159), custom_call_target="InvertDiagBlocksLowerTriangular" | custom-call | tf_op jit(solution)/shard_map/jit(cholesky)/cholesky | solution.py:34
  414.3 11.7 %cholesky.299 = f32[128,128]{1,0:T(8,128)S(1)} custom-call(f32[128,128]{1,0:T(8,128)S(1)} %convolution_subtract_fusion.15), custom_call_target="Cholesky" | custom-call | tf_op jit(solution)/shard_map/jit(cholesky)/cholesky | solution.py:34
  426.1 0.6 compare_reduce_fusion.2
  426.7 0.6 compare_reduce_fusion.3
  429.1 4.2 while.21
  429.7 1.4 dynamic-slice.45
  431.8 1.4 dynamic-slice.45
  433.4 19.9 %custom-call.39 = f32[2,128,128]{1,2,0:T(8,128)S(1)} custom-call(f32[2,128,128]{2,1,0:T(8,128)S(1)} %get-tuple-element.81), custom_call_target="InvertDiagBlocksLowerTriangular" | custom-call | tf_op jit(solution)/shard_map/triangular_solve/custom-call.6 | solution.py:21
  455.1 0.6 copy-done.9
  456.9 11.7 %cholesky.316 = f32[128,128]{1,0:T(8,128)S(1)} custom-call(f32[128,128]{1,0:T(8,128)S(1)} %cholesky.355), custom_call_target="Cholesky" | custom-call | tf_op jit(solution)/shard_map/jit(cholesky)/cholesky | solution.py:28
  468.7 9.8 %custom-call.41 = f32[1,128,128]{1,2,0:T(8,128)S(1)} custom-call(f32[1,128,128]{2,1,0:T(8,128)S(1)} %get-tuple-element.155), custom_call_target="InvertDiagBlocksLowerTriangular" | custom-call | tf_op jit(solution)/shard_map/jit(cholesky)/cholesky | solution.py:28
  478.9 11.9 %cholesky.333 = f32[128,128]{1,0:T(8,128)S(1)} custom-call(f32[128,128]{1,0:T(8,128)S(1)} %convolution_subtract_fusion.14), custom_call_target="Cholesky" | custom-call | tf_op jit(solution)/shard_map/jit(cholesky)/cholesky | solution.py:28
  490.9 0.6 compare_reduce_fusion
  491.6 0.6 compare_reduce_fusion.1
  493.6 4.0 while.22
  494.2 1.4 bitcast_dynamic-update-slice_fusion.11
  496.2 1.4 bitcast_dynamic-update-slice_fusion.11
  497.6 19.7 %custom-call.43 = f32[2,128,128]{1,2,0:T(8,128)S(1)} custom-call(f32[2,128,128]{2,1,0:T(8,128)S(1)} %get-tuple-element.84), custom_call_target="InvertDiagBlocksLowerTriangular" | custom-call | tf_op jit(solution)/shard_map/triangular_solve/custom-call.5 | solution.py:21
  521.2 0.7 copy-done.13
  522.5 1.4 convolution_subtract_fusion
  524.5 1.4 convolution_subtract_fusion.1
  (140 shorter events, 23.1 us)
Async XLA Ops:
  7.2 60.7 %all-reduce.10.cloned.1.call-start = ((), (), s32[]{:S(2)}) async-start(), calls=%async_computation | async-start | bytes 524288 | tf_op jit(solution)/shard_map/psum | solution.py:11
  7.2 1.0 slice-start
  9.1 96.6 %all-reduce.12.cloned.1.call-start = ((), (), s32[]{:S(2)}) async-start(), calls=%async_computation.1 | async-start | bytes 524288 | tf_op jit(solution)/shard_map/psum | solution.py:49
  70.0 0.9 copy-start
  70.1 140.2 %all-reduce.18.cloned.1.call-start = ((), (), s32[]{:S(2)}) async-start(), calls=%async_computation.4 | async-start | bytes 1310720 | tf_op jit(solution)/shard_map/psum | solution.py:49
  105.6 1.2 copy-start.4
  167.2 1.0 copy-start.3
  169.6 1.0 copy-start.1
  169.6 151.6 %all-reduce.16.cloned.1.call-start = ((), (), s32[]{:S(2)}) async-start(), calls=%async_computation.3 | async-start | bytes 1572864 | tf_op jit(solution)/shard_map/psum | solution.py:54
  210.2 1.3 copy-start.11
  274.5 1.0 copy-start.6
  277.6 113.5 %all-reduce.14.cloned.1.call-start = ((), (), s32[]{:S(2)}) async-start(), calls=%async_computation.2 | async-start | bytes 3145728 | tf_op jit(solution)/shard_map/psum | solution.py:69
  322.2 1.3 copy-start.7
  327.2 1.0 copy-start.2
  391.0 1.2 copy-start.5
  429.1 24.1 %copy-start.10 = (f32[256,256]{1,0:T(8,128)S(1)}, f32[256,256]{1,0:T(8,128)}, u32[]{:S(2)}) copy-start(f32[256,256]{1,0:T(8,128)} %get-tuple-element.137) | copy-start | bytes 786436
  454.8 1.0 copy-start.9
  519.3 1.0 copy-start.8
  521.0 1.0 copy-start.13
  522.5 1.4 copy-start.12
Sparse Core Ops, SparseCore 0:
  11.6 56.2 all-reduce.9
  70.9 34.6 all-reduce.11
  169.7 40.4 all-reduce.17
  277.7 43.4 all-reduce.15
  331.2 59.7 all-reduce.13
where the time goes:
time: 542 us; the launch traced here: 533 us
  waiting for transfers between devices  233 us (43%)
  other arithmetic  220 us (41%)
  matrix products  31.4 us (6%)
  local copies, waits for them, and re-layouts  26.9 us (5%)
  between operations  20.3 us (4%)
    another operation x9, other arithmetic, tri_solve(): lax.linalg.triangular_solve(factor, values, left_side=on_left, lower=True...  79 us
    psum x2, waiting for transfers between devices, local(): lax.psum((product(panel.T, panel), panel * top_flag), 'row')  72.2 us
    another operation x14, other arithmetic, inverse_of(): factor = jnp.linalg.cholesky(normal)  69.4 us
    psum x1, waiting for transfers between devices, local(): lax.psum((product(a_left, strip_masked.T), product(b_left, strip_masked.T...  59.9 us
    psum x1, waiting for transfers between devices, broadcast(): return lax.psum(block, axis)  58.8 us
    psum x1, waiting for transfers between devices, local(): lax.psum((product(w_rows.T, a_matrix), product(w_rows.T, b_matrix)), 'row')  42.4 us
    another operation x7, other arithmetic, lower_from_reversed(): factor = jnp.linalg.cholesky(gram[::-1, ::-1])  34.6 us
    another operation x6, other arithmetic, local(): factor = jnp.linalg.cholesky(gram)  34 us
  transfers between devices with their start and end apart: 5, of which 5 were waited for; matrix products, arithmetic and copies ran while one was open for 1% of the time, Pallas kernels for 0%

commit v1 on v0

--- a/solution.py
+++ b/solution.py
@@ -8,7 +8,7 @@
 
 def broadcast(block, axis, source):
     block = jnp.where(lax.axis_index(axis) == source, block, jnp.zeros_like(block))
-    return lax.psum(block, axis)
+    return jnp.sum(lax.all_gather(block, axis), axis=0)
 
 
 def product(left_side, right_side):

time: 542 us -> 521 us (0.961)
  waiting for transfers between devices: 233 us -> 212 us
    all_gather x0 -> x2, waiting for transfers between devices: none -> 65.3 us  [broadcast(): return jnp.sum(lax.all_gather(block, axis), axis=0)]
    psum x1 -> x0, waiting for transfers between devices: 58.8 us -> none  [broadcast(): return lax.psum(block, axis)]
    psum x2 -> x1, waiting for transfers between devices: 72.2 us -> 34.7 us  [local(): lax.psum((product(panel.T, panel), panel * top_flag), 'row')]
    psum x1, waiting for transfers between devices: 42.4 us -> 52.4 us  [local(): lax.psum((product(w_rows.T, a_matrix), product(w_rows.T, b_matrix)), 'row')]
where the time goes in v1:
time: 521 us; the launch traced here: 512 us
  other arithmetic  223 us (43%)
  waiting for transfers between devices  212 us (41%)
  matrix products  31.2 us (6%)
  local copies, waits for them, and re-layouts  24.5 us (5%)
  between operations  20 us (4%)
    another operation x9, other arithmetic, tri_solve(): lax.linalg.triangular_solve(factor, values, left_side=on_left, lower=True...  79.2 us
    another operation x14, other arithmetic, inverse_of(): factor = jnp.linalg.cholesky(normal)  69.3 us
    all_gather x2, waiting for transfers between devices, broadcast(): return jnp.sum(lax.all_gather(block, axis), axis=0)  65.3 us
    psum x1, waiting for transfers between devices, local(): lax.psum((product(a_left, strip_masked.T), product(b_left, strip_masked.T...  59.5 us
    psum x1, waiting for transfers between devices, local(): lax.psum((product(w_rows.T, a_matrix), product(w_rows.T, b_matrix)), 'row')  52.4 us
    psum x1, waiting for transfers between devices, local(): lax.psum((product(panel.T, panel), panel * top_flag), 'row')  34.7 us
    another operation x7, other arithmetic, lower_from_reversed(): factor = jnp.linalg.cholesky(gram[::-1, ::-1])  34.6 us
    another operation x6, other arithmetic, local(): factor = jnp.linalg.cholesky(gram)  34 us
  transfers between devices with their start and end apart: 5, of which 5 were waited for; matrix products, arithmetic and copies ran while one was open for 1% of the time, Pallas kernels for 0%

profile of v1, /device:TPU:0, one launch (start us, length us, event | category | flops | bytes accessed | tf_op | source)
XLA Modules:
  0.0 511.6 jit_solution(12211430557152174929)
XLA Ops:
  7.2 1.0 slice.96
  8.3 0.7 broadcast_select_fusion.1
  9.1 32.3 %all-gather.5.cloned.1.call-done = f32[2048,256]{0,1:T(8,128)} async-done(((f32[256,256]{0,1:T(8,128)}), f32[2048,256]{0,1:T(8,128)}) %all-gather.5.cloned.1.call-update) | async-done | bytes 2097168 | tf_op jit(solution)/shard_map/all_gather | solution.py:11
  41.4 2.5 copy.22
  44.4 1.1 fusion.99
  45.6 0.7 broadcast_multiply_fusion.1
  46.3 34.7 %all-reduce.7.cloned.1.call-done = f32[256,256]{0,1:T(8,128)} async-done(((f32[256,256]{0,1:T(8,128)}), f32[256,256]{0,1:T(8,128)}) %all-reduce.7.cloned.1.call-update) | async-done | bytes 262160 | tf_op jit(solution)/shard_map/psum | solution.py:49
  81.0 1.1 copy.6
  82.1 1.0 fusion.18
  83.1 11.7 %cholesky.214 = f32[128,128]{1,0:T(8,128)S(1)} custom-call(f32[128,128]{1,0:T(8,128)S(1)} %cholesky.346), custom_call_target="Cholesky" | custom-call | tf_op jit(solution)/shard_map/jit(cholesky)/cholesky | solution.py:50
  94.8 9.8 %custom-call.32 = f32[1,128,128]{1,2,0:T(8,128)S(1)} custom-call(f32[1,128,128]{2,1,0:T(8,128)S(1)} %get-tuple-element.166), custom_call_target="InvertDiagBlocksLowerTriangular" | custom-call | tf_op jit(solution)/shard_map/jit(cholesky)/cholesky | solution.py:50
  105.2 11.7 %cholesky.231 = f32[128,128]{1,0:T(8,128)S(1)} custom-call(f32[128,128]{1,0:T(8,128)S(1)} %convolution_subtract_fusion.17), custom_call_target="Cholesky" | custom-call | tf_op jit(solution)/shard_map/jit(cholesky)/cholesky | solution.py:50
  116.9 0.7 compare_reduce_fusion.6
  119.1 4.6 while.19
  120.2 1.4 bitcast_dynamic-update-slice_fusion.8
  122.3 1.4 bitcast_dynamic-update-slice_fusion.8
  123.7 19.7 %custom-call.33 = f32[2,128,128]{1,2,0:T(8,128)S(1)} custom-call(f32[2,128,128]{2,1,0:T(8,128)S(1)} %get-tuple-element.77), custom_call_target="InvertDiagBlocksLowerTriangular" | custom-call | tf_op jit(solution)/shard_map/triangular_solve/custom-call.0 | solution.py:21
  144.3 1.4 fusion.94
  145.7 1.4 fusion.93
  147.1 52.4 %all-reduce.11.cloned.1.call-done = (f32[256,384]{1,0:T(8,128)}, f32[256,256]{0,1:T(8,128)}, f32[256,384]{1,0:T(8,128)}) async-done(((f32[256,384]{1,0:T(8,128)}, f32[256,256]{0,1:T(8,128)}, f32[256,384]{1,0:T(8,128)}), (f32[256,384]{1,0:T(8,128)}, f32[256,256]{0,1:T(8,128)}, f32[256,384]{1,0:T(8,128)})) %all-reduce.11.cloned.1.call-update) | async-done | bytes 1048592 | tf_op jit(solution)/shard_map/psum | solution.py:54
  199.5 1.2 fusion.46
  200.7 1.2 convolution_subtract_fusion.12
  202.8 11.7 %cholesky.248 = f32[128,128]{1,0:T(8,128)S(1)} custom-call(f32[128,128]{1,0:T(8,128)S(1)} %cholesky.349), custom_call_target="Cholesky" | custom-call | tf_op jit(solution)/shard_map/jit(cholesky)/cholesky | solution.py:28
  214.6 9.8 %custom-call.35 = f32[1,128,128]{1,2,0:T(8,128)S(1)} custom-call(f32[1,128,128]{2,1,0:T(8,128)S(1)} %get-tuple-element.162), custom_call_target="InvertDiagBlocksLowerTriangular" | custom-call | tf_op jit(solution)/shard_map/jit(cholesky)/cholesky | solution.py:28
  224.9 11.7 %cholesky.265 = f32[128,128]{1,0:T(8,128)S(1)} custom-call(f32[128,128]{1,0:T(8,128)S(1)} %convolution_subtract_fusion.16), custom_call_target="Cholesky" | custom-call | tf_op jit(solution)/shard_map/jit(cholesky)/cholesky | solution.py:28
  236.7 0.6 compare_reduce_fusion.4
  237.3 0.6 compare_reduce_fusion.5
  239.3 4.2 while.20
  240.1 1.4 bitcast_dynamic-update-slice_fusion.9
  242.1 1.4 bitcast_dynamic-update-slice_fusion.9
  243.5 19.7 %custom-call.37 = f32[2,128,128]{1,2,0:T(8,128)S(1)} custom-call(f32[2,128,128]{2,1,0:T(8,128)S(1)} %get-tuple-element.80), custom_call_target="InvertDiagBlocksLowerTriangular" | custom-call | tf_op jit(solution)/shard_map/triangular_solve/custom-call.5 | solution.py:21
  265.6 1.4 broadcast_select_fusion
  267.1 1.1 fusion.1
  268.8 0.6 convolution_subtract_fusion.3
  269.4 1.1 fusion.5
  270.5 33.1 %all-gather.7.cloned.1.call-done = f32[1024,384]{1,0:T(8,128)} async-done(((f32[256,384]{1,0:T(8,128)}), f32[1024,384]{1,0:T(8,128)}) %all-gather.7.cloned.1.call-update) | async-done | bytes 1572880 | tf_op jit(solution)/shard_map/all_gather | solution.py:11
  303.6 1.5 reduce_sum.19
  305.2 1.3 fusion.102
  307.1 1.3 fusion.100
  308.4 1.1 fusion.3
  309.5 1.7 rev.6
  311.3 59.5 %all-reduce.9.cloned.1.call-done = (f32[256,256]{0,1:T(8,128)}, f32[256,256]{1,0:T(8,128)}, f32[256,256]{0,1:T(8,128)}, f32[256,256]{1,0:T(8,128)}, f32[256,256]{0,1:T(8,128)}, /*index=5*/f32[256,256]{1,0:T(8,128)}) async-done(((f32[256,256]{0,1:T(8,128)}, f32[256,256]{1,0:T(8,128)}, f32[256,256]{0,1:T(8,128)}, f32[256,256]{1,0:T(8,128)}, f32[256,256]{0,1:T(8,128)}, /*index=5*/f32[256,256]{1,0:T(8,128)}), ...) | async-done | bytes 1572880 | tf_op jit(solution)/shard_map/psum | solution.py:69
  370.9 1.1 copy.9
  371.9 1.0 fusion.16
  372.9 11.7 %cholesky.282 = f32[128,128]{1,0:T(8,128)S(1)} custom-call(f32[128,128]{1,0:T(8,128)S(1)} %cholesky.352), custom_call_target="Cholesky" | custom-call | tf_op jit(solution)/shard_map/jit(cholesky)/cholesky | solution.py:34
  384.7 9.8 %custom-call.38 = f32[1,128,128]{1,2,0:T(8,128)S(1)} custom-call(f32[1,128,128]{2,1,0:T(8,128)S(1)} %get-tuple-element.158), custom_call_target="InvertDiagBlocksLowerTriangular" | custom-call | tf_op jit(solution)/shard_map/jit(cholesky)/cholesky | solution.py:34
  395.0 11.7 %cholesky.299 = f32[128,128]{1,0:T(8,128)S(1)} custom-call(f32[128,128]{1,0:T(8,128)S(1)} %convolution_subtract_fusion.15), custom_call_target="Cholesky" | custom-call | tf_op jit(solution)/shard_map/jit(cholesky)/cholesky | solution.py:34
  406.8 0.6 compare_reduce_fusion.2
  407.4 0.6 compare_reduce_fusion.3
  409.8 4.2 while.21
  410.4 1.4 dynamic-slice.45
  412.5 1.4 dynamic-slice.45
  414.1 20.1 %custom-call.39 = f32[2,128,128]{1,2,0:T(8,128)S(1)} custom-call(f32[2,128,128]{2,1,0:T(8,128)S(1)} %get-tuple-element.81), custom_call_target="InvertDiagBlocksLowerTriangular" | custom-call | tf_op jit(solution)/shard_map/triangular_solve/custom-call.6 | solution.py:21
  437.1 11.7 %cholesky.316 = f32[128,128]{1,0:T(8,128)S(1)} custom-call(f32[128,128]{1,0:T(8,128)S(1)} %cholesky.355), custom_call_target="Cholesky" | custom-call | tf_op jit(solution)/shard_map/jit(cholesky)/cholesky | solution.py:28
  448.9 9.8 %custom-call.41 = f32[1,128,128]{1,2,0:T(8,128)S(1)} custom-call(f32[1,128,128]{2,1,0:T(8,128)S(1)} %get-tuple-element.154), custom_call_target="InvertDiagBlocksLowerTriangular" | custom-call | tf_op jit(solution)/shard_map/jit(cholesky)/cholesky | solution.py:28
  459.2 11.9 %cholesky.333 = f32[128,128]{1,0:T(8,128)S(1)} custom-call(f32[128,128]{1,0:T(8,128)S(1)} %convolution_subtract_fusion.14), custom_call_target="Cholesky" | custom-call | tf_op jit(solution)/shard_map/jit(cholesky)/cholesky | solution.py:28
  471.1 0.6 compare_reduce_fusion
  471.7 0.6 compare_reduce_fusion.1
  473.7 4.0 while.22
  474.4 1.4 bitcast_dynamic-update-slice_fusion.11
  476.4 1.4 bitcast_dynamic-update-slice_fusion.11
  477.8 19.7 %custom-call.43 = f32[2,128,128]{1,2,0:T(8,128)S(1)} custom-call(f32[2,128,128]{2,1,0:T(8,128)S(1)} %get-tuple-element.84), custom_call_target="InvertDiagBlocksLowerTriangular" | custom-call | tf_op jit(solution)/shard_map/triangular_solve/custom-call.5 | solution.py:21
  501.5 1.4 convolution_subtract_fusion
  503.5 1.4 convolution_subtract_fusion.1
  (132 shorter events, 21.6 us)
Async XLA Ops:
  7.2 34.2 %all-gather.5.cloned.1.call-start = ((), (), s32[]{:S(2)}) async-start(), calls=%async_computation.1 | async-start | bytes 2359296 | tf_op jit(solution)/shard_map/all_gather | solution.py:11
  9.1 71.9 %all-reduce.7.cloned.1.call-start = ((), (), s32[]{:S(2)}) async-start(), calls=%async_computation | async-start | bytes 524288 | tf_op jit(solution)/shard_map/psum | solution.py:49
  45.5 154.0 %all-reduce.11.cloned.1.call-start = ((), (), s32[]{:S(2)}) async-start(), calls=%async_computation.4 | async-start | bytes 2097152 | tf_op jit(solution)/shard_map/psum | solution.py:54
  83.1 61.2 %copy-start = (f32[256,384]{1,0:T(8,128)S(1)}, f32[256,384]{1,0:T(8,128)}, u32[]{:S(2)}) copy-start(f32[256,384]{1,0:T(8,128)} %param.11) | copy-start | bytes 1179652
  104.9 40.8 %copy-start.1 = (f32[256,384]{1,0:T(8,128)S(1)}, f32[256,384]{1,0:T(8,128)}, u32[]{:S(2)}) copy-start(f32[256,384]{1,0:T(8,128)} %param.12) | copy-start | bytes 1179652
  147.1 156.5 %all-gather.7.cloned.1.call-start = ((), (), s32[]{:S(2)}) async-start(), calls=%async_computation.2 | async-start | bytes 1966080 | tf_op jit(solution)/shard_map/all_gather | solution.py:11
  224.6 40.3 %copy-start.3 = (f32[256,384]{1,0:T(8,128)S(1)}, f32[256,384]{1,0:T(8,128)}, u32[]{:S(2)}) copy-start(f32[256,384]{1,0:T(8,128)} %get-tuple-element.142) | copy-start | bytes 1179652
  264.7 3.5 copy-start.2
  267.0 103.9 %all-reduce.9.cloned.1.call-start = ((), (), s32[]{:S(2)}) async-start(), calls=%async_computation.3 | async-start | bytes 3145728 | tf_op jit(solution)/shard_map/psum | solution.py:69
  394.7 39.4 %copy-start.6 = (f32[256,256]{1,0:T(8,128)S(1)}, f32[256,256]{1,0:T(8,128)}, u32[]{:S(2)}) copy-start(f32[256,256]{1,0:T(8,128)} %get-tuple-element.137) | copy-start | bytes 786436
  409.8 26.2 %copy-start.5 = (f32[256,256]{1,0:T(8,128)S(1)}, f32[256,256]{1,0:T(8,128)}, u32[]{:S(2)}) copy-start(f32[256,256]{1,0:T(8,128)} %get-tuple-element.139) | copy-start | bytes 786436
  473.7 26.1 %copy-start.4 = (f32[256,256]{1,0:T(8,128)S(1)}, f32[256,256]{1,0:T(8,128)}, u32[]{:S(2)}) copy-start(f32[256,256]{1,0:T(8,128)} %get-tuple-element.135) | copy-start | bytes 786436
  497.8 3.1 copy-start.8
  499.5 3.3 copy-start.7
Sparse Core Ops, SparseCore 0:
  10.4 30.8 all-gather.4
  45.6 35.2 all-reduce.6
  147.2 52.2 all-reduce.10
  267.1 36.4 all-gather.6
  311.4 59.3 all-reduce.8
